TPU v7x, 128 devices: a whole 4x4x4 slice. The times are simulated.
128 devices in a mesh: dp: 64 (over y, x, z), feat: 2 (over core).
Axes of the slice: x: 4, y: 4, z: 4, core: 2. Of those that a mesh axis runs over, the one named last changes fastest.
Arguments:
- view_one: float32 [1024, 8192], P('dp', 'feat'), may hold values from -30 to 30, as said below
- view_two: float32 [1024, 8192], P('dp', 'feat'), may hold values from -30 to 30, as said below
- loss_scale: float32 [1], replicated, may hold values from 512 to 4096
Outputs:
- grad_one: float32 [1024, 8192], P('dp', 'feat')
- grad_two: float32 [1024, 8192], P('dp', 'feat')
Inputs may be any that keep to these rules, and one draw needn't show every extreme that they name: `view_one`: float embeddings. `view_two`: float embeddings.
All inputs are finite; a program needn't handle non-finite values.
Results may differ from a plain program's by a relative error of at most 0.008.
Values may be sent and summed in bfloat16 or wider, within the bound.
A program may use at most 128 MiB of HBM per device.

v0:
```python
import jax
import jax.numpy as jnp
from jax import lax
from jax.sharding import PartitionSpec as P

eps_value = 1e-05
offdiag_weight = 0.0051


def finish_samples(grad_blk, normal_loc, scale_loc, total):
    back = lax.all_to_all(
        grad_blk.astype(jnp.bfloat16), "dp", split_axis=0, concat_axis=1, tiled=True
    ).astype(grad_blk.dtype)
    weight = lax.psum(jnp.sum(back * normal_loc, axis=0), "dp") / total
    return scale_loc * (back - normal_loc * weight)


def shards(view_one, view_two, loss_scale):
    local_rows, half_width = view_one.shape
    blocks = lax.axis_size("dp")
    total = local_rows * blocks
    narrow = half_width // blocks
    row_tile = lax.axis_index("dp")
    core_index = lax.axis_index("feat")
    sums = lax.psum((jnp.sum(view_one, axis=0), jnp.sum(view_two, axis=0)), "dp")
    centre_one = view_one - sums[0] / total
    centre_two = view_two - sums[1] / total
    squares = lax.psum(
        (jnp.sum(centre_one * centre_one, axis=0), jnp.sum(centre_two * centre_two, axis=0)), "dp"
    )
    var_one = squares[0] / total
    var_two = squares[1] / total
    inverse_one = lax.rsqrt(var_one + eps_value)
    inverse_two = lax.rsqrt(var_two + eps_value)
    normal_one = (centre_one * inverse_one).astype(jnp.bfloat16)
    normal_two = (centre_two * inverse_two).astype(jnp.bfloat16)
    rows_mine = lax.all_to_all(normal_one, "dp", split_axis=1, concat_axis=0, tiled=True)
    rows_both = lax.all_gather(rows_mine, "feat", axis=1, tiled=True)
    columns = lax.all_gather(normal_two, "dp", axis=0, tiled=True)
    corr = (
        lax.dot_general(
            rows_both, columns, (((0,), (0,)), ((), ())), preferred_element_type=jnp.float32
        )
        / total
    )
    row_index = jnp.arange(2 * narrow)
    row_feature = jnp.where(
        row_index < narrow,
        row_tile * narrow + row_index,
        half_width + row_tile * narrow + row_index - narrow,
    )
    col_feature = core_index * half_width + jnp.arange(half_width)
    on_diag = row_feature[:, None] == col_feature[None, :]
    grad_tile = (
        loss_scale[0] * jnp.where(on_diag, 2.0 * (corr - 1.0), 2.0 * offdiag_weight * corr)
    ).astype(jnp.bfloat16)
    row_terms = (
        lax.dot_general(
            columns, grad_tile, (((1,), (1,)), ((), ())), preferred_element_type=jnp.float32
        )
        / total
    )
    grad_rows = lax.psum_scatter(
        row_terms.astype(jnp.bfloat16), "feat", scatter_dimension=1, tiled=True
    ).astype(jnp.float32)
    grad_one = finish_samples(grad_rows, normal_one.astype(jnp.float32), inverse_one, total)
    grad_cols = lax.psum_scatter(
        jnp.dot(rows_both, grad_tile, preferred_element_type=jnp.float32) / total,
        "dp",
        scatter_dimension=0,
        tiled=True,
    )
    normal_loc = normal_two.astype(jnp.float32)
    weight_two = lax.psum(jnp.sum(grad_cols * normal_loc, axis=0), "dp") / total
    grad_two = inverse_two * (grad_cols - normal_loc * weight_two)
    return (grad_one, grad_two)


def solution(mesh):
    placed = (P("dp", "feat"), P("dp", "feat"), P())
    return jax.shard_map(
        shards,
        mesh=mesh,
        in_specs=placed,
        out_specs=(P("dp", "feat"), P("dp", "feat")),
        check_vma=False,
    )
```

profile of v0, /device:TPU:0, one launch (start us, length us, event | category | flops | bytes accessed | tf_op | source)
XLA Modules:
  0.0 1542.8 jit_solution(5023275016394404803)
XLA Ops:
  7.2 0.0 copy-start.1
  7.2 0.0 all-gather.2.cloned.1.call-start
  7.2 1.0 reduce_sum.54
  8.2 1.0 reduce_sum.56
  9.2 350.2 %all-reduce.2 = (f32[4096]{0:T(1024)S(1)}, f32[4096]{0:T(1024)S(1)}) all-reduce(f32[4096]{0:T(1024)S(1)} %reduce_sum.56, f32[4096]{0:T(1024)S(1)} %reduce_sum.54), channel_id=1, replica_groups=mesh['dp'=64,'feat'=2] {'dp'}, use_global_device_ids=true, to_apply=%region_5.0 | all-reduce | flops 8192 | bytes 65536 | tf_op jit(solution)/shard_map/psum | solution.py:25
  359.5 1.0 multiply_reduce_fusion
  360.5 1.0 multiply_reduce_fusion.1
  361.5 341.5 %all-reduce.1 = (f32[4096]{0:T(1024)S(1)}, f32[4096]{0:T(1024)S(1)}) all-reduce(f32[4096]{0:T(1024)S(1)} %multiply_reduce_fusion, f32[4096]{0:T(1024)S(1)} %multiply_reduce_fusion.1), channel_id=1, replica_groups=mesh['dp'=64,'feat'=2] {'dp'}, use_global_device_ids=true, to_apply=%region_7.0 | all-reduce | flops 8192 | bytes 65536 | tf_op jit(solution)/shard_map/psum | solution.py:28
  703.0 1.6 multiply_convert_fusion.8
  704.6 0.0 all-gather.2.cloned.1.call-update
  704.7 0.0 copy-done.1
  704.7 0.2 all_to_all.24
  705.0 0.2 copy.16
  705.2 0.8 reshape.33
  706.0 4.6 all-to-all-start
  710.6 0.0 reduce-scatter.3.cloned.1.call-start
  711.4 9.4 all-to-all-done
  720.8 0.2 reshape.34
  721.0 0.1 copy.12
  721.1 2.0 all_gather.7
  723.1 53.8 %all-gather.2.cloned.1.call-done = bf16[1024,4096]{1,0:T(8,128)(2,1)} async-done(((bf16[16,4096]{1,0:T(8,128)(2,1)}), bf16[1024,4096]{1,0:T(8,128)(2,1)}) %all-gather.2.cloned.1.call-update) | async-done | bytes 8388624 | tf_op jit(solution)/shard_map/all_gather | solution.py:39
  776.9 0.0 copy-start
  776.9 4.8 fusion.33
  781.7 1.0 copy-done
  782.7 3.7 fusion.4
  786.3 0.0 reduce-scatter.3.cloned.1.call-update
  786.4 0.0 reduce-scatter.5.cloned.1.call-start
  786.4 8.2 convolution_multiply_fusion
  794.6 0.0 reduce-scatter.5.cloned.1.call-update
  794.7 1.6 reduce-scatter.3.cloned.1.call-done
  796.3 1.1 copy.13
  797.3 0.0 copy-start.2
  797.4 0.2 reshape.35
  797.6 21.0 %all_to_all.32 = bf16[64,2,512]{2,1,0:T(2,128)(2,1)S(1)} all-to-all(bf16[64,2,512]{2,1,0:T(2,128)(2,1)S(1)} %reshape.35), channel_id=1, replica_groups=mesh['dp'=64,'feat'=2] {'dp'}, dimensions={0} | all-to-all | bytes 262144 | tf_op jit(solution)/shard_map/all_to_all | solution.py:11
  818.6 0.2 reshape.36
  818.8 0.2 copy.14
  819.0 0.2 reshape.32
  819.2 0.1 fusion.19
  819.3 371.2 %reduce-scatter.5.cloned.1.call-done = f32[16,4096]{1,0:T(8,128)} async-done(((f32[1024,4096]{1,0:T(8,128)}), f32[16,4096]{1,0:T(8,128)}) %reduce-scatter.5.cloned.1.call-update) | async-done | bytes 262160 | tf_op jit(solution)/shard_map/reduce_scatter | solution.py:67
  1190.5 0.0 copy-done.2
  1190.5 1.0 fusion.22
  1191.5 342.3 %all-reduce = (f32[4096]{0:T(1024)S(1)}, f32[4096]{0:T(1024)S(1)}) all-reduce(f32[4096]{0:T(1024)S(1)} %fusion.19, f32[4096]{0:T(1024)S(1)} %fusion.22), channel_id=1, replica_groups=mesh['dp'=64,'feat'=2] {'dp'}, use_global_device_ids=true, to_apply=%region_10.11 | all-reduce | flops 8192 | bytes 65536 | tf_op jit(solution)/shard_map/psum | solution.py:14
  1533.8 0.8 fusion.21
  1534.6 1.7 fusion.24
  (9 shorter events, 0.1 us)
Async XLA Ops:
  7.2 697.5 %copy-start.1 = (f32[16,4096]{1,0:T(8,128)S(1)}, f32[16,4096]{1,0:T(8,128)}, u32[]{:S(2)}) copy-start(f32[16,4096]{1,0:T(8,128)} %param.3) | copy-start | bytes 786436
  7.2 769.7 %all-gather.2.cloned.1.call-start = ((), (), s32[]{:S(2)}) async-start(), calls=%async_computation.4 | async-start | bytes 8519680 | tf_op jit(solution)/shard_map/all_gather | solution.py:39
  706.0 14.8 all-to-all-start
  710.6 85.6 %reduce-scatter.3.cloned.1.call-start = ((), (), s32[]{:S(2)}) async-start(), calls=%async_computation.5 | async-start | bytes 393216 | tf_op jit(solution)/shard_map/reduce_scatter | solution.py:63
  776.9 5.8 copy-start
  786.4 404.1 %reduce-scatter.5.cloned.1.call-start = ((), (), s32[]{:S(2)}) async-start(), calls=%async_computation.6 | async-start | bytes 17039360 | tf_op jit(solution)/shard_map/reduce_scatter | solution.py:67
  797.3 393.1 %copy-start.2 = (f32[16,4096]{1,0:T(8,128)S(1)}, f32[16,4096]{1,0:T(8,128)}, u32[]{:S(2)}) copy-start(f32[16,4096]{1,0:T(8,128)} %param.4) | copy-start | bytes 786436
Sparse Core Ops, SparseCore 0:
  704.8 72.0 all-gather.1
  786.5 9.7 reduce-scatter.2
  798.8 391.6 reduce-scatter.4
where the time goes:
time: 1540 us
  blocking collectives  1060 us (69%)
  waiting for transfers between devices  436 us (28%)
  matrix products  16.7 us (1%)
    reduce_scatter x1, waiting for transfers between devices, shards(): lax.psum_scatter(jnp.dot(rows_both, grad_tile, preferred_element_type=jnp...  371 us
    psum x1, blocking collectives, shards(): lax.psum((jnp.sum(view_one, axis=0), jnp.sum(view_two, axis=0)), 'dp')  350 us
    psum x1, blocking collectives, finish_samples(): weight = lax.psum(jnp.sum(back * normal_loc, axis=0), 'dp') / total  342 us
    psum x1, blocking collectives, shards(): lax.psum((jnp.sum(centre_one * centre_one, axis=0), jnp.sum(centre_two *...  342 us
    all_gather x1, waiting for transfers between devices, shards(): columns = lax.all_gather(normal_two, 'dp', axis=0, tiled=True)  53.8 us
  transfers between devices with their start and end apart: 4, of which 4 were waited for; matrix products, arithmetic and copies ran while one was open for 1% of the time, Pallas kernels for 0%

commit v1 on v0

v1 whole, which is shorter than its diff:
```python
import jax
import jax.numpy as jnp
from jax import lax
from jax.experimental import pallas as pl
from jax.experimental.pallas import tpu as pltpu
from jax.sharding import PartitionSpec as P

MESH = pl.DeviceIdType.MESH
F32, BF16 = jnp.float32, jnp.bfloat16

eps_value = 1e-05
offdiag_weight = 0.0051

CHIPS, CORES = 64, 2
SAMPLES, ROWS, WIDE, TILE = 1024, 16, 4096, 128
BLOCKS = [(r, c) for r in range(8) for c in range(r, 8)]
PART = len(BLOCKS) * TILE // 3
THIRD, FINE = PART // 4, PART // 16
ORDERS = ((4, 16, 1), (16, 1, 4), (1, 4, 16))


def remote(src, dst, send_sem, recv_sem, chip, core):
    return pltpu.make_async_remote_copy(
        src_ref=src, dst_ref=dst, send_sem=send_sem, recv_sem=recv_sem, device_id=(chip, core), device_id_type=MESH
    )


def rows_at(start, size):
    return pl.ds(pl.multiple_of(start, 16), size)


def lanes_at(tile):
    return pl.ds(pl.multiple_of(tile * TILE, TILE), TILE)


def coordinate(chip, stride):
    return (chip // stride) % 4


def partner(chip, stride, hop):
    here = coordinate(chip, stride)
    return chip + ((here + hop) % 4 - here) * stride


def kernel(
    one, two, scale_ref, out, held, own, other, inv_own, inv_other, part, got_a, sum_a, got_b, sum_b, got_c, full, gram, grads,
    in_send, in_recv, out_send, out_recv, pair_send, pair_recv, ring_send, ring_recv, local_sem,
):
    chip, core = lax.axis_index("dp"), lax.axis_index("feat")
    half, tile = chip // 32, chip % 32
    mine = half == core

    barrier = pltpu.get_barrier_semaphore()

    @pl.loop(1, CHIPS * CORES)
    def _(k):
        flat = (chip * CORES + core + k) % (CHIPS * CORES)
        pl.semaphore_signal(barrier, inc=1, device_id=(flat // CORES, flat % CORES), device_id_type=MESH)

    pl.semaphore_wait(barrier, CHIPS * CORES - 1)

    def to_owner(t, view, target_core):
        chip_to = 32 * core + t
        return remote(
            view.at[:, lanes_at(t)], held.at[rows_at(chip * ROWS, ROWS), :],
            in_send.at[2 * t + target_core], in_recv.at[chip], chip_to, target_core,
        )

    def stays(t, target_core):
        return jnp.logical_and(32 * core + t == chip, core == target_core)

    @pl.loop(0, 32)
    def _(k):
        t = (k + chip) % 32
        for target_core, view in enumerate((one, two)):
            @pl.when(jnp.logical_not(stays(t, target_core)))
            def _():
                to_owner(t, view, target_core).start()

            @pl.when(stays(t, target_core))
            def _():
                pltpu.make_async_copy(view.at[:, lanes_at(t)], held.at[rows_at(chip * ROWS, ROWS), :], local_sem).start()

    @pl.when(mine)
    def _():
        pltpu.make_async_copy(one.at[:, lanes_at(tile)], held.at[rows_at(chip * ROWS, ROWS), :], local_sem).wait()

    @pl.loop(0, CHIPS)
    def _(i):
        @pl.when(jnp.logical_not(jnp.logical_and(i == chip, mine)))
        def _():
            rows = held.at[rows_at(i * ROWS, ROWS), :]
            remote(rows, rows, in_send.at[0], in_recv.at[i], chip, core).wait_recv()

    values = held[...]
    centre = values - jnp.sum(values, axis=0, keepdims=True) / SAMPLES
    variance = jnp.sum(centre * centre, axis=0, keepdims=True) / SAMPLES
    inverse = lax.rsqrt(variance + eps_value)
    own[...] = (centre * inverse).astype(BF16)
    inv_own[...] = jnp.broadcast_to(inverse, inv_own.shape)
    swap = remote(own, other, pair_send.at[0], pair_recv.at[0], chip, 1 - core)
    swap_inv = remote(inv_own, inv_other, pair_send.at[1], pair_recv.at[1], chip, 1 - core)
    swap.start()
    swap_inv.start()

    for r in range(8):
        panel = lax.dot_general(
            own[r * TILE:(r + 1) * TILE, :], own[r * TILE:, :], (((1,), (1,)), ((), ())), preferred_element_type=F32
        )
        for c in range(r, 8):
            at = BLOCKS.index((r, c)) * TILE
            part[at:at + TILE, :] = panel[:, (c - r) * TILE:(c - r + 1) * TILE].astype(BF16)

    def step(phase, p, hop, src, dst):
        stride = ORDERS[p][(0, 1, 2, 1, 0)[phase]]
        at = (phase * 3 + p) * 3 + hop - 1
        return remote(src, dst, ring_send.at[at], ring_recv.at[at], partner(chip, stride, hop), core)

    def first(p, hop):
        to = (coordinate(chip, ORDERS[p][0]) + hop) % 4
        return step(0, p, hop, part.at[rows_at(p * PART + to * THIRD, THIRD), :], got_a.at[p, hop - 1])

    def second(p, hop):
        to = (coordinate(chip, ORDERS[p][1]) + hop) % 4
        return step(1, p, hop, sum_a.at[p, rows_at(to * FINE, FINE), :], got_b.at[p, hop - 1])

    def third(p, hop):
        return step(2, p, hop, sum_b.at[p], got_c.at[p, hop - 1])

    def fine_rows(p):
        start = p * PART + coordinate(chip, ORDERS[p][0]) * THIRD + coordinate(chip, ORDERS[p][1]) * FINE
        return rows_at(start, FINE)

    def third_rows(p):
        return rows_at(p * PART + coordinate(chip, ORDERS[p][0]) * THIRD, THIRD)

    def fourth(p, hop):
        return step(3, p, hop, full.at[fine_rows(p), :], full.at[fine_rows(p), :])

    def fifth(p, hop):
        return step(4, p, hop, full.at[third_rows(p), :], full.at[third_rows(p), :])

    HOPS = (2, 1, 3)
    for p in range(3):
        for hop in HOPS:
            first(p, hop).start()
    for p in range(3):
        for hop in HOPS:
            first(p, hop).wait_recv()
        total = part[third_rows(p), :].astype(F32)
        for hop in HOPS:
            total = total + got_a[p, hop - 1].astype(F32)
        sum_a[p] = total.astype(BF16)
        for hop in HOPS:
            second(p, hop).start()
    for p in range(3):
        for hop in HOPS:
            second(p, hop).wait_recv()
        total = sum_a[p, rows_at(coordinate(chip, ORDERS[p][1]) * FINE, FINE), :].astype(F32)
        for hop in HOPS:
            total = total + got_b[p, hop - 1].astype(F32)
        sum_b[p] = total.astype(BF16)
        for hop in HOPS:
            third(p, hop).start()
    for p in range(3):
        for hop in HOPS:
            third(p, hop).wait_recv()
        total = sum_b[p].astype(F32)
        for hop in HOPS:
            total = total + got_c[p, hop - 1].astype(F32)
        full[fine_rows(p), :] = total.astype(BF16)
        for hop in HOPS:
            fourth(p, hop).start()
    for p in range(3):
        for hop in HOPS:
            fourth(p, hop).wait_recv()
        for hop in HOPS:
            fifth(p, hop).start()

    swap.wait_recv()
    swap_inv.wait_recv()
    theirs = other[...].astype(F32)
    ours = own[...].astype(F32)
    scale = scale_ref[0]
    corr = jnp.sum(ours * theirs, axis=0, keepdims=True) / SAMPLES
    diagonal = scale * (2.0 * (corr - 1.0) - 2.0 * offdiag_weight * corr)

    for p in range(3):
        for hop in HOPS:
            fifth(p, hop).wait_recv()
    for at, (r, c) in enumerate(BLOCKS):
        block = full[at * TILE:(at + 1) * TILE, :]
        gram[r * TILE:(r + 1) * TILE, c * TILE:(c + 1) * TILE] = block
        if r != c:
            gram[c * TILE:(c + 1) * TILE, r * TILE:(r + 1) * TILE] = block.T
    back = jnp.dot(gram[...], other[...], preferred_element_type=F32) * (scale * (2.0 * offdiag_weight / (SAMPLES * SAMPLES)))
    back = back + ours * (diagonal / SAMPLES)
    weight = jnp.sum(back * theirs, axis=0, keepdims=True) / SAMPLES
    grads[...] = (inv_other[0:1, :] * (back - theirs * weight)).astype(BF16)

    def to_samples(i):
        return remote(
            grads.at[rows_at(i * ROWS, ROWS), :], out.at[1 - core, :, lanes_at(tile)],
            out_send.at[i], out_recv.at[2 * tile + core], i, half,
        )

    @pl.loop(0, CHIPS)
    def _(k):
        i = (k + chip) % CHIPS
        stay = jnp.logical_and(i == chip, mine)

        @pl.when(jnp.logical_not(stay))
        def _():
            to_samples(i).start()

        @pl.when(stay)
        def _():
            pltpu.make_async_copy(grads.at[rows_at(i * ROWS, ROWS), :], out.at[1 - core, :, lanes_at(tile)], local_sem).start()

    @pl.when(mine)
    def _():
        pltpu.make_async_copy(
            grads.at[rows_at(chip * ROWS, ROWS), :], out.at[1 - core, :, lanes_at(tile)], local_sem
        ).wait()

    @pl.loop(0, 32)
    def _(t):
        for from_core in range(2):
            @pl.when(jnp.logical_not(stays(t, from_core)))
            def _():
                remote(
                    grads.at[rows_at(0, ROWS), :], out.at[1 - from_core, :, lanes_at(t)],
                    out_send.at[0], out_recv.at[2 * t + from_core], chip, core,
                ).wait_recv()

    swap.wait_send()
    swap_inv.wait_send()
    for p in range(3):
        for hop in HOPS:
            for send in (first, second, third, fourth, fifth):
                send(p, hop).wait_send()

    @pl.loop(0, 32)
    def _(t):
        for target_core, view in enumerate((one, two)):
            @pl.when(jnp.logical_not(stays(t, target_core)))
            def _():
                to_owner(t, view, target_core).wait_send()

    @pl.loop(0, CHIPS)
    def _(i):
        @pl.when(jnp.logical_not(jnp.logical_and(i == chip, mine)))
        def _():
            to_samples(i).wait_send()


def shards(view_one, view_two, loss_scale):
    out = pl.pallas_call(
        kernel,
        out_shape=jax.ShapeDtypeStruct((2, ROWS, WIDE), BF16),
        in_specs=[
            pl.BlockSpec(memory_space=pl.ANY),
            pl.BlockSpec(memory_space=pl.ANY),
            pl.BlockSpec(memory_space=pltpu.SMEM),
        ],
        out_specs=pl.BlockSpec(memory_space=pltpu.VMEM),
        scratch_shapes=[
            pltpu.VMEM((SAMPLES, TILE), F32),
            pltpu.VMEM((SAMPLES, TILE), BF16),
            pltpu.VMEM((SAMPLES, TILE), BF16),
            pltpu.VMEM((8, TILE), F32),
            pltpu.VMEM((8, TILE), F32),
            pltpu.VMEM((3 * PART, TILE), BF16),
            pltpu.VMEM((3, 3, THIRD, TILE), BF16),
            pltpu.VMEM((3, THIRD, TILE), BF16),
            pltpu.VMEM((3, 3, FINE, TILE), BF16),
            pltpu.VMEM((3, FINE, TILE), BF16),
            pltpu.VMEM((3, 3, FINE, TILE), BF16),
            pltpu.VMEM((3 * PART, TILE), BF16),
            pltpu.VMEM((SAMPLES, SAMPLES), BF16),
            pltpu.VMEM((SAMPLES, TILE), BF16),
            pltpu.SemaphoreType.DMA((CHIPS,)),
            pltpu.SemaphoreType.DMA((CHIPS,)),
            pltpu.SemaphoreType.DMA((CHIPS,)),
            pltpu.SemaphoreType.DMA((CHIPS,)),
            pltpu.SemaphoreType.DMA((2,)),
            pltpu.SemaphoreType.DMA((2,)),
            pltpu.SemaphoreType.DMA((45,)),
            pltpu.SemaphoreType.DMA((45,)),
            pltpu.SemaphoreType.DMA,
        ],
        compiler_params=pltpu.CompilerParams(
            collective_id=0, has_side_effects=True, vmem_limit_bytes=40 * 1024 * 1024
        ),
    )(view_one, view_two, loss_scale)
    return out[0].astype(F32), out[1].astype(F32)


def solution(mesh):
    placed = (P("dp", "feat"), P("dp", "feat"), P())
    return jax.shard_map(
        shards,
        mesh=mesh,
        in_specs=placed,
        out_specs=(P("dp", "feat"), P("dp", "feat")),
        check_vma=False,
    )
```

time: 1540 us -> 62.7 us (0.04)
  the two profiles are of different devices: /device:TPU:0 before, /device:TPU:1 now
where the time goes in v1:
time: 62.7 us; the launch traced here: 62.5 us
  Pallas kernels  58.5 us (93%)
  local copies, waits for them, and re-layouts  1.89 us (3%)
  between operations  1.29 us (2%)
  other arithmetic  0.83 us (1%)
    pallas_call x1, Pallas kernels, shards(): pl.pallas_call(kernel, out_shape=jax.ShapeDtypeStruct((2, ROWS, WIDE), BF...  58.5 us
    unnamed x4, local copies, waits for them, and re-layouts  1.89 us

profile of v1, /device:TPU:1, one launch (start us, length us, event | category | flops | bytes accessed | tf_op | source)
XLA Modules:
  0.0 62.5 jit_solution(6076964855080778266)
XLA Ops:
  1.3 0.0 copy-start
  1.3 0.9 %copy-done = f32[16,4096]{1,0:T(8,128)S(1)} copy-done((f32[16,4096]{1,0:T(8,128)S(1)}, f32[16,4096]{1,0:T(8,128)}, u32[]{:S(2)}) %copy-start) | copy-done | bytes 262168
  2.2 0.0 copy-start.1
  2.2 0.9 %copy-done.1 = f32[16,4096]{1,0:T(8,128)S(1)} copy-done((f32[16,4096]{1,0:T(8,128)S(1)}, f32[16,4096]{1,0:T(8,128)}, u32[]{:S(2)}) %copy-start.1) | copy-done | bytes 262168
  3.2 58.5 %shard_map.50 = bf16[2,16,4096]{2,1,0:T(8,128)(2,1)S(1)} custom-call(f32[16,4096]{1,0:T(8,128)S(1)} %copy-done, f32[16,4096]{1,0:T(8,128)S(1)} %copy-done.1, f32[1]{0:T(128)S(6)} %copy.5.scale_ref), custom_call_target="tpu_custom_call" | custom-call | tf_op jit(solution)/shard_map/pallas_call | solution.py:258
  61.7 0.8 %bitcast_convert_fusion = (f32[16,4096]{1,0:T(8,128)}, f32[16,4096]{1,0:T(8,128)}) fusion(bf16[2,16,4096]{2,1,0:T(8,128)(2,1)S(1)} %shard_map.50), kind=kLoop, calls=%fused_computation | loop fusion | flops 131072 | bytes 786432 | tf_op jit(solution)/shard_map/convert_element_type | solution.py:296
Async XLA Ops:
  1.3 1.0 %copy-start = (f32[16,4096]{1,0:T(8,128)S(1)}, f32[16,4096]{1,0:T(8,128)}, u32[]{:S(2)}) copy-start(f32[16,4096]{1,0:T(8,128)} %one.1) | copy-start | bytes 786436
  2.2 0.9 %copy-start.1 = (f32[16,4096]{1,0:T(8,128)S(1)}, f32[16,4096]{1,0:T(8,128)}, u32[]{:S(2)}) copy-start(f32[16,4096]{1,0:T(8,128)} %two.1) | copy-start | bytes 786436

commit v2 on v0

v2 whole, which is shorter than its diff:
```python
import jax
import jax.numpy as jnp
from jax import lax
from jax.experimental import pallas as pl
from jax.experimental.pallas import tpu as pltpu
from jax.sharding import PartitionSpec as P

MESH = pl.DeviceIdType.MESH
F32, BF16 = jnp.float32, jnp.bfloat16

eps_value = 1e-05
offdiag_weight = 0.0051

CHIPS = 64
SAMPLES, ROWS, WIDE, TILE = 1024, 16, 4096, 128
BLOCKS = [(r, c) for r in range(8) for c in range(r, 8)]
WAVES = 2
CHAINS = 3 * WAVES
PART = len(BLOCKS) * TILE // CHAINS
CHUNK, FINE = PART // 4, PART // 16
ORDERS = ((4, 16, 1), (16, 1, 4), (1, 4, 16))
HOPS = (2, 1, 3)
PHASES = 5


def apart(shift):
    return min(shift, 4 - shift)


SHIFTS = sorted(
    ((y, x, z) for y in range(4) for x in range(4) for z in range(4)), key=lambda s: -(apart(s[0]) + apart(s[1]) + apart(s[2]))
)
PLANE = [(x, z) for y, x, z in SHIFTS if y == 0]


def remote(src, dst, send_sem, recv_sem, chip, core):
    return pltpu.make_async_remote_copy(
        src_ref=src, dst_ref=dst, send_sem=send_sem, recv_sem=recv_sem, device_id=(chip, core), device_id_type=MESH
    )


def rows_at(start, size):
    return pl.ds(pl.multiple_of(start, 16), size)


def lanes_at(tile):
    return pl.ds(pl.multiple_of(tile * TILE, TILE), TILE)


def coordinate(chip, stride):
    return (chip // stride) % 4


def partner(chip, stride, hop):
    here = coordinate(chip, stride)
    return chip + ((here + hop) % 4 - here) * stride


def kernel(
    one, two, scale_hbm, out, held, own, other, inv_own, inv_other, part, got_a, sum_a, got_b, sum_b, got_c, full, gram, grads,
    scale_ref, in_send, in_recv, out_send, out_recv, pair_send, pair_recv, ring_send, ring_recv, local_sem, scale_sem,
):
    chip, core = lax.axis_index("dp"), lax.axis_index("feat")
    half, tile = chip // 32, chip % 32
    mine = half == core
    not_mine = jnp.logical_not(mine)
    at_y, at_x, at_z = coordinate(chip, 16), coordinate(chip, 4), coordinate(chip, 1)

    def shifted(shift):
        y, x, z = shift
        return (at_y + y) % 4 * 16 + (at_x + x) % 4 * 4 + (at_z + z) % 4

    barrier = pltpu.get_barrier_semaphore()
    for shift in SHIFTS[:-1]:
        pl.semaphore_signal(barrier, inc=1, device_id=(shifted(shift), half), device_id_type=MESH)

    @pl.when(not_mine)
    def _():
        pl.semaphore_signal(barrier, inc=1, device_id=(chip, half), device_id_type=MESH)

    scale_copy = pltpu.make_async_copy(scale_hbm, scale_ref, scale_sem)
    scale_copy.start()

    @pl.when(mine)
    def _():
        pl.semaphore_wait(barrier, CHIPS - 1)

    @pl.when(not_mine)
    def _():
        pl.semaphore_wait(barrier, CHIPS)

    my_rows = held.at[rows_at(chip * ROWS, ROWS), :]

    def to_owner(view, chip_to, core_to):
        return remote(view.at[:, lanes_at(chip_to % 32)], my_rows, in_send, in_recv, chip_to, core_to)

    for x, z in PLANE[:-1]:
        for y in range(2):
            chip_to = (2 * core + y) * 16 + (at_x + x) % 4 * 4 + (at_z + z) % 4
            to_owner(one, chip_to, 0).start()
            to_owner(two, chip_to, 1).start()
    for y in range(2):
        chip_to = (2 * core + y) * 16 + at_x * 4 + at_z
        for core_to, view in enumerate((one, two)):
            stays = jnp.logical_and(chip_to == chip, core == core_to)

            @pl.when(jnp.logical_not(stays))
            def _():
                to_owner(view, chip_to, core_to).start()

            @pl.when(stays)
            def _():
                pltpu.make_async_copy(view.at[:, lanes_at(tile)], my_rows, local_sem).start()

    def all_of(ref, count, send_sem, recv_sem):
        rows = ref.at[0:count * ROWS, :]
        return remote(rows, rows, send_sem, recv_sem, chip, core)

    def local_in():
        return pltpu.make_async_copy(one.at[:, lanes_at(tile)], my_rows, local_sem)

    @pl.when(mine)
    def _():
        all_of(held, CHIPS - 1, in_send, in_recv).wait_recv()
        local_in().wait()

    @pl.when(not_mine)
    def _():
        all_of(held, CHIPS, in_send, in_recv).wait_recv()

    values = held[...]
    centre = values - jnp.sum(values, axis=0, keepdims=True) / SAMPLES
    variance = jnp.sum(centre * centre, axis=0, keepdims=True) / SAMPLES
    inverse = lax.rsqrt(variance + eps_value)
    own[...] = (centre * inverse).astype(BF16)
    inv_own[...] = jnp.broadcast_to(inverse, inv_own.shape)
    swap = remote(own, other, pair_send.at[0], pair_recv.at[0], chip, 1 - core)
    swap_inv = remote(inv_own, inv_other, pair_send.at[1], pair_recv.at[1], chip, 1 - core)

    def step(phase, q, hop, src, dst):
        stride = ORDERS[q % 3][(0, 1, 2, 1, 0)[phase]]
        at = (phase * CHAINS + q) * 3 + hop - 1
        return remote(src, dst, ring_send.at[at], ring_recv.at[at], partner(chip, stride, hop), core)

    def first(q, hop):
        to = (coordinate(chip, ORDERS[q % 3][0]) + hop) % 4
        return step(0, q, hop, part.at[rows_at(q * PART + to * CHUNK, CHUNK), :], got_a.at[q, hop - 1])

    def second(q, hop):
        to = (coordinate(chip, ORDERS[q % 3][1]) + hop) % 4
        return step(1, q, hop, sum_a.at[q, rows_at(to * FINE, FINE), :], got_b.at[q, hop - 1])

    def third(q, hop):
        return step(2, q, hop, sum_b.at[q], got_c.at[q, hop - 1])

    def chunk_rows(q):
        return rows_at(q * PART + coordinate(chip, ORDERS[q % 3][0]) * CHUNK, CHUNK)

    def fine_rows(q):
        start = q * PART + coordinate(chip, ORDERS[q % 3][0]) * CHUNK + coordinate(chip, ORDERS[q % 3][1]) * FINE
        return rows_at(start, FINE)

    def fourth(q, hop):
        return step(3, q, hop, full.at[fine_rows(q), :], full.at[fine_rows(q), :])

    def fifth(q, hop):
        return step(4, q, hop, full.at[chunk_rows(q), :], full.at[chunk_rows(q), :])

    def chains(wave):
        return range(3 * wave, 3 * wave + 3)

    def start(phase, q):
        for hop in HOPS:
            phase(q, hop).start()

    def arrived(phase, q):
        for hop in HOPS:
            phase(q, hop).wait_recv()

    def summed(mine_ref, got, q):
        total = mine_ref.astype(F32)
        for hop in HOPS:
            total = total + got[q, hop - 1].astype(F32)
        return total.astype(BF16)


    def sent_in():
        @pl.when(mine)
        def _():
            all_of(held, CHIPS - 1, in_send, in_recv).wait_send()

        @pl.when(not_mine)
        def _():
            all_of(held, CHIPS, in_send, in_recv).wait_send()

    swap.start()
    swap_inv.start()

    for wave in range(WAVES):
        blocks = list(enumerate(BLOCKS))[wave * 36 // WAVES:(wave + 1) * 36 // WAVES]
        for r in range(8):
            columns = [c for _, (row, c) in blocks if row == r]
            if columns:
                panel = lax.dot_general(
                    own[r * TILE:(r + 1) * TILE, :], own[columns[0] * TILE:(columns[-1] + 1) * TILE, :],
                    (((1,), (1,)), ((), ())), preferred_element_type=F32,
                )
                for at, (row, c) in blocks:
                    if row == r:
                        lanes = slice((c - columns[0]) * TILE, (c - columns[0] + 1) * TILE)
                        part[at * TILE:(at + 1) * TILE, :] = panel[:, lanes].astype(BF16)
        for q in chains(wave):
            start(first, q)

    sent_in()
    swap.wait()
    swap_inv.wait()
    scale_copy.wait()
    scale = scale_ref[0]
    corr = jnp.sum(own[...].astype(F32) * other[...].astype(F32), axis=0, keepdims=True) / SAMPLES
    diagonal = scale * (2.0 * (corr - 1.0) - 2.0 * offdiag_weight * corr)

    for wave in range(WAVES):
        for q in chains(wave):
            arrived(first, q)
            sum_a[q] = summed(part[chunk_rows(q), :], got_a, q)
            start(second, q)
    for wave in range(WAVES):
        for q in chains(wave):
            arrived(second, q)
            sum_b[q] = summed(sum_a[q, rows_at(coordinate(chip, ORDERS[q % 3][1]) * FINE, FINE), :], got_b, q)
            start(third, q)
    for wave in range(WAVES):
        for q in chains(wave):
            arrived(third, q)
            full[fine_rows(q), :] = summed(sum_b[q], got_c, q)
            start(fourth, q)
    for wave in range(WAVES):
        for q in chains(wave):
            arrived(fourth, q)
            start(fifth, q)

    for wave in range(WAVES):
        for q in chains(wave):
            arrived(fifth, q)
        for at, (r, c) in list(enumerate(BLOCKS))[wave * 36 // WAVES:(wave + 1) * 36 // WAVES]:
            block = full[at * TILE:(at + 1) * TILE, :]
            gram[r * TILE:(r + 1) * TILE, c * TILE:(c + 1) * TILE] = block
            if r != c:
                gram[c * TILE:(c + 1) * TILE, r * TILE:(r + 1) * TILE] = block.T
    theirs = other[...].astype(F32)
    back = jnp.dot(gram[...], other[...], preferred_element_type=F32) * (scale * (2.0 * offdiag_weight / (SAMPLES * SAMPLES)))
    back = back + own[...].astype(F32) * (diagonal / SAMPLES)
    weight = jnp.sum(back * theirs, axis=0, keepdims=True) / SAMPLES
    grads[...] = (inv_other[0:1, :] * (back - theirs * weight)).astype(BF16)

    place = out.at[1 - core, :, lanes_at(tile)]

    def to_samples(chip_to):
        return remote(grads.at[rows_at(chip_to * ROWS, ROWS), :], place, out_send, out_recv, chip_to, half)

    for shift in SHIFTS[:-1]:
        to_samples(shifted(shift)).start()

    @pl.when(not_mine)
    def _():
        to_samples(chip).start()

    @pl.when(mine)
    def _():
        pltpu.make_async_copy(grads.at[rows_at(chip * ROWS, ROWS), :], place, local_sem).start()

    for phase in (first, second, third, fourth, fifth):
        for q in range(CHAINS):
            for hop in HOPS:
                phase(q, hop).wait_send()

    @pl.when(mine)
    def _():
        all_of(grads, CHIPS - 1, out_send, out_recv).wait()
        pltpu.make_async_copy(grads.at[rows_at(chip * ROWS, ROWS), :], place, local_sem).wait()

    @pl.when(not_mine)
    def _():
        all_of(grads, CHIPS, out_send, out_recv).wait()


def shards(view_one, view_two, loss_scale):
    hbm = pl.BlockSpec(memory_space=pltpu.HBM)
    out = pl.pallas_call(
        kernel,
        out_shape=jax.ShapeDtypeStruct((2, ROWS, WIDE), BF16),
        in_specs=[hbm, hbm, hbm],
        out_specs=pl.BlockSpec(memory_space=pltpu.VMEM),
        scratch_shapes=[
            pltpu.VMEM((SAMPLES, TILE), F32),
            pltpu.VMEM((SAMPLES, TILE), BF16),
            pltpu.VMEM((SAMPLES, TILE), BF16),
            pltpu.VMEM((8, TILE), F32),
            pltpu.VMEM((8, TILE), F32),
            pltpu.VMEM((CHAINS * PART, TILE), BF16),
            pltpu.VMEM((CHAINS, 3, CHUNK, TILE), BF16),
            pltpu.VMEM((CHAINS, CHUNK, TILE), BF16),
            pltpu.VMEM((CHAINS, 3, FINE, TILE), BF16),
            pltpu.VMEM((CHAINS, FINE, TILE), BF16),
            pltpu.VMEM((CHAINS, 3, FINE, TILE), BF16),
            pltpu.VMEM((CHAINS * PART, TILE), BF16),
            pltpu.VMEM((SAMPLES, SAMPLES), BF16),
            pltpu.VMEM((SAMPLES, TILE), BF16),
            pltpu.SMEM((1,), F32),
            pltpu.SemaphoreType.DMA,
            pltpu.SemaphoreType.DMA,
            pltpu.SemaphoreType.DMA,
            pltpu.SemaphoreType.DMA,
            pltpu.SemaphoreType.DMA((2,)),
            pltpu.SemaphoreType.DMA((2,)),
            pltpu.SemaphoreType.DMA((PHASES * CHAINS * 3,)),
            pltpu.SemaphoreType.DMA((PHASES * CHAINS * 3,)),
            pltpu.SemaphoreType.DMA,
            pltpu.SemaphoreType.DMA,
        ],
        compiler_params=pltpu.CompilerParams(
            collective_id=0, has_side_effects=True, vmem_limit_bytes=60 * 1024 * 1024
        ),
    )(view_one, view_two, loss_scale)
    return out[0].astype(F32), out[1].astype(F32)


def solution(mesh):
    placed = (P("dp", "feat"), P("dp", "feat"), P())
    return jax.shard_map(
        shards,
        mesh=mesh,
        in_specs=placed,
        out_specs=(P("dp", "feat"), P("dp", "feat")),
        check_vma=False,
    )
```

time: 1540 us -> 54 us (0.04)
  the two profiles are of different devices: /device:TPU:0 before, /device:TPU:1 now
where the time goes in v2:
time: 54 us; the launch traced here: 53.9 us
  Pallas kernels  50.8 us (94%)
  other arithmetic  1.79 us (3%)
  between operations  1.28 us (2%)
    pallas_call x1, Pallas kernels, shards(): pl.pallas_call(kernel, out_shape=jax.ShapeDtypeStruct((2, ROWS, WIDE), BF...  50.8 us
    convert_element_type x1, other arithmetic, shards(): return (out[0].astype(F32), out[1].astype(F32))  1.79 us

profile of v2, /device:TPU:1, one launch (start us, length us, event | category | flops | bytes accessed | tf_op | source)
XLA Modules:
  0.0 53.9 jit_solution(13332046577967753552)
XLA Ops:
  1.3 50.8 %shard_map.50 = bf16[2,16,4096]{2,1,0:T(8,128)(2,1)} custom-call(f32[16,4096]{1,0:T(8,128)} %one.1, f32[16,4096]{1,0:T(8,128)} %two.1, f32[1]{0:T(128)S(6)} %copy.5.scale_hbm), custom_call_target="tpu_custom_call" | custom-call | tf_op jit(solution)/shard_map/pallas_call | solution.py:290
  52.1 1.8 %bitcast_convert_fusion = (f32[16,4096]{1,0:T(8,128)}, f32[16,4096]{1,0:T(8,128)}) fusion(bf16[2,16,4096]{2,1,0:T(8,128)(2,1)} %shard_map.50), kind=kLoop, calls=%fused_computation | loop fusion | flops 131072 | bytes 786432 | tf_op jit(solution)/shard_map/convert_element_type | solution.py:326

commit v3 on v2

--- a/solution.py
+++ b/solution.py
@@ -57,8 +57,8 @@
 
 
 def kernel(
-    one, two, scale_hbm, out, held, own, other, inv_own, inv_other, part, got_a, sum_a, got_b, sum_b, got_c, full, gram, grads,
-    scale_ref, in_send, in_recv, out_send, out_recv, pair_send, pair_recv, ring_send, ring_recv, local_sem, scale_sem,
+    one, two, scale_hbm, out, views, means, rests, held, held_means, own, other, inv_own, inv_other, part, got_a, sum_a, got_b, sum_b, got_c, full, gram, grads,
+    scale_ref, in_send, in_recv, mean_send, mean_recv, out_send, out_recv, pair_send, pair_recv, ring_send, ring_recv, local_sem, view_sem, scale_sem,
 ):
     chip, core = lax.axis_index("dp"), lax.axis_index("feat")
     half, tile = chip // 32, chip % 32
@@ -70,6 +70,10 @@
         y, x, z = shift
         return (at_y + y) % 4 * 16 + (at_x + x) % 4 * 4 + (at_z + z) % 4
 
+    loads = [pltpu.make_async_copy(view, views.at[k], view_sem.at[k]) for k, view in enumerate((one, two))]
+    for load in loads:
+        load.start()
+
     barrier = pltpu.get_barrier_semaphore()
     for shift in SHIFTS[:-1]:
         pl.semaphore_signal(barrier, inc=1, device_id=(shifted(shift), half), device_id_type=MESH)
@@ -81,6 +85,14 @@
     scale_copy = pltpu.make_async_copy(scale_hbm, scale_ref, scale_sem)
     scale_copy.start()
 
+    for k, load in enumerate(loads):
+        load.wait()
+        samples = views[k]
+        block_mean = jnp.sum(samples, axis=0, keepdims=True) / ROWS
+        rests[k] = (samples - block_mean).astype(BF16)
+        for t in range(WIDE // TILE):
+            means[k, t] = block_mean[:, t * TILE:(t + 1) * TILE]
+
     @pl.when(mine)
     def _():
         pl.semaphore_wait(barrier, CHIPS - 1)
@@ -91,45 +103,62 @@
 
     my_rows = held.at[rows_at(chip * ROWS, ROWS), :]
 
-    def to_owner(view, chip_to, core_to):
-        return remote(view.at[:, lanes_at(chip_to % 32)], my_rows, in_send, in_recv, chip_to, core_to)
+    def to_owner(chip_to, core_to):
+        t = chip_to % 32
+        return (
+            remote(means.at[core_to, t], held_means.at[chip], mean_send, mean_recv, chip_to, core_to),
+            remote(rests.at[core_to, :, lanes_at(t)], my_rows, in_send, in_recv, chip_to, core_to),
+        )
+
+    def stay_here():
+        return (
+            pltpu.make_async_copy(means.at[core, tile], held_means.at[chip], local_sem.at[0]),
+            pltpu.make_async_copy(rests.at[core, :, lanes_at(tile)], my_rows, local_sem.at[1]),
+        )
 
     for x, z in PLANE[:-1]:
         for y in range(2):
             chip_to = (2 * core + y) * 16 + (at_x + x) % 4 * 4 + (at_z + z) % 4
-            to_owner(one, chip_to, 0).start()
-            to_owner(two, chip_to, 1).start()
+            for core_to in range(2):
+                for copy in to_owner(chip_to, core_to):
+                    copy.start()
     for y in range(2):
         chip_to = (2 * core + y) * 16 + at_x * 4 + at_z
-        for core_to, view in enumerate((one, two)):
+        for core_to in range(2):
             stays = jnp.logical_and(chip_to == chip, core == core_to)
 
             @pl.when(jnp.logical_not(stays))
             def _():
-                to_owner(view, chip_to, core_to).start()
+                for copy in to_owner(chip_to, core_to):
+                    copy.start()
 
             @pl.when(stays)
             def _():
-                pltpu.make_async_copy(view.at[:, lanes_at(tile)], my_rows, local_sem).start()
+                for copy in stay_here():
+                    copy.start()
 
     def all_of(ref, count, send_sem, recv_sem):
-        rows = ref.at[0:count * ROWS, :]
+        rows = ref.at[0:count]
         return remote(rows, rows, send_sem, recv_sem, chip, core)
 
-    def local_in():
-        return pltpu.make_async_copy(one.at[:, lanes_at(tile)], my_rows, local_sem)
+    def all_in(count):
+        return all_of(held_means, count, mean_send, mean_recv), all_of(held, count * ROWS, in_send, in_recv)
 
     @pl.when(mine)
     def _():
-        all_of(held, CHIPS - 1, in_send, in_recv).wait_recv()
-        local_in().wait()
-
-    @pl.when(not_mine)
-    def _():
-        all_of(held, CHIPS, in_send, in_recv).wait_recv()
-
-    values = held[...]
-    centre = values - jnp.sum(values, axis=0, keepdims=True) / SAMPLES
+        for copy in all_in(CHIPS - 1):
+            copy.wait_recv()
+        for copy in stay_here():
+            copy.wait()
+
+    @pl.when(not_mine)
+    def _():
+        for copy in all_in(CHIPS):
+            copy.wait_recv()
+
+    block_means = held_means[...]
+    offsets = block_means - jnp.sum(block_means, axis=0, keepdims=True) / CHIPS
+    centre = (held[...].astype(F32).reshape(CHIPS, ROWS, TILE) + offsets).reshape(SAMPLES, TILE)
     variance = jnp.sum(centre * centre, axis=0, keepdims=True) / SAMPLES
     inverse = lax.rsqrt(variance + eps_value)
     own[...] = (centre * inverse).astype(BF16)
@@ -187,11 +216,13 @@
     def sent_in():
         @pl.when(mine)
         def _():
-            all_of(held, CHIPS - 1, in_send, in_recv).wait_send()
+            for copy in all_in(CHIPS - 1):
+                copy.wait_send()
 
         @pl.when(not_mine)
         def _():
-            all_of(held, CHIPS, in_send, in_recv).wait_send()
+            for copy in all_in(CHIPS):
+                copy.wait_send()
 
     swap.start()
     swap_inv.start()
@@ -268,7 +299,7 @@
 
     @pl.when(mine)
     def _():
-        pltpu.make_async_copy(grads.at[rows_at(chip * ROWS, ROWS), :], place, local_sem).start()
+        pltpu.make_async_copy(grads.at[rows_at(chip * ROWS, ROWS), :], place, local_sem.at[0]).start()
 
     for phase in (first, second, third, fourth, fifth):
         for q in range(CHAINS):
@@ -277,12 +308,12 @@
 
     @pl.when(mine)
     def _():
-        all_of(grads, CHIPS - 1, out_send, out_recv).wait()
-        pltpu.make_async_copy(grads.at[rows_at(chip * ROWS, ROWS), :], place, local_sem).wait()
-
-    @pl.when(not_mine)
-    def _():
-        all_of(grads, CHIPS, out_send, out_recv).wait()
+        all_of(grads, (CHIPS - 1) * ROWS, out_send, out_recv).wait()
+        pltpu.make_async_copy(grads.at[rows_at(chip * ROWS, ROWS), :], place, local_sem.at[0]).wait()
+
+    @pl.when(not_mine)
+    def _():
+        all_of(grads, CHIPS * ROWS, out_send, out_recv).wait()
 
 
 def shards(view_one, view_two, loss_scale):
@@ -293,7 +324,11 @@
         in_specs=[hbm, hbm, hbm],
         out_specs=pl.BlockSpec(memory_space=pltpu.VMEM),
         scratch_shapes=[
-            pltpu.VMEM((SAMPLES, TILE), F32),
+            pltpu.VMEM((2, ROWS, WIDE), F32),
+            pltpu.VMEM((2, WIDE // TILE, 1, TILE), F32),
+            pltpu.VMEM((2, ROWS, WIDE), BF16),
+            pltpu.VMEM((SAMPLES, TILE), BF16),
+            pltpu.VMEM((CHIPS, 1, TILE), F32),
             pltpu.VMEM((SAMPLES, TILE), BF16),
             pltpu.VMEM((SAMPLES, TILE), BF16),
             pltpu.VMEM((8, TILE), F32),
@@ -312,15 +347,18 @@
             pltpu.SemaphoreType.DMA,
             pltpu.SemaphoreType.DMA,
             pltpu.SemaphoreType.DMA,
+            pltpu.SemaphoreType.DMA,
+            pltpu.SemaphoreType.DMA,
             pltpu.SemaphoreType.DMA((2,)),
             pltpu.SemaphoreType.DMA((2,)),
             pltpu.SemaphoreType.DMA((PHASES * CHAINS * 3,)),
             pltpu.SemaphoreType.DMA((PHASES * CHAINS * 3,)),
-            pltpu.SemaphoreType.DMA,
+            pltpu.SemaphoreType.DMA((2,)),
+            pltpu.SemaphoreType.DMA((2,)),
             pltpu.SemaphoreType.DMA,
         ],
         compiler_params=pltpu.CompilerParams(
-            collective_id=0, has_side_effects=True, vmem_limit_bytes=60 * 1024 * 1024
+            collective_id=0, has_side_effects=True, vmem_limit_bytes=54848 * 1024
         ),
     )(view_one, view_two, loss_scale)
     return out[0].astype(F32), out[1].astype(F32)

time: 54 us -> 49.9 us (0.924)
  Pallas kernels: 50.8 us -> 47.6 us
  other arithmetic: 1.79 us -> 0.83 us
    pallas_call x1, Pallas kernels: 50.8 us -> 47.6 us  [shards(): pl.pallas_call(kernel, out_shape=jax.ShapeDtypeStruct((2, ROWS, WIDE), BF...]
    convert_element_type x1, other arithmetic: 1.79 us -> 0.83 us  [shards(): return (out[0].astype(F32), out[1].astype(F32))]
where the time goes in v3:
time: 49.9 us; the launch traced here: 49.7 us
  Pallas kernels  47.6 us (95%)
  between operations  1.28 us (3%)
  other arithmetic  0.83 us (2%)
    pallas_call x1, Pallas kernels, shards(): pl.pallas_call(kernel, out_shape=jax.ShapeDtypeStruct((2, ROWS, WIDE), BF...  47.6 us

profile of v3, /device:TPU:1, one launch (start us, length us, event | category | flops | bytes accessed | tf_op | source)
XLA Modules:
  0.0 49.7 jit_solution(5085564164109625238)
XLA Ops:
  1.3 47.6 %shard_map.50 = bf16[2,16,4096]{2,1,0:T(8,128)(2,1)S(1)} custom-call(f32[16,4096]{1,0:T(8,128)} %one.1, f32[16,4096]{1,0:T(8,128)} %two.1, f32[1]{0:T(128)S(6)} %copy.5.scale_hbm), custom_call_target="tpu_custom_call" | custom-call | tf_op jit(solution)/shard_map/pallas_call | solution.py:321
  48.9 0.8 %bitcast_convert_fusion = (f32[16,4096]{1,0:T(8,128)}, f32[16,4096]{1,0:T(8,128)}) fusion(bf16[2,16,4096]{2,1,0:T(8,128)(2,1)S(1)} %shard_map.50), kind=kLoop, calls=%fused_computation | loop fusion | flops 131072 | bytes 786432 | tf_op jit(solution)/shard_map/convert_element_type | solution.py:364

commit v4 on v3

--- a/solution.py
+++ b/solution.py
@@ -14,8 +14,9 @@
 CHIPS = 64
 SAMPLES, ROWS, WIDE, TILE = 1024, 16, 4096, 128
 BLOCKS = [(r, c) for r in range(8) for c in range(r, 8)]
-WAVES = 2
+WAVES = 3
 CHAINS = 3 * WAVES
+WHOLE = [0] + [min(r for r, c in BLOCKS[wave * 36 // WAVES:] + [(8, 8)]) * TILE for wave in range(1, WAVES + 1)]
 PART = len(BLOCKS) * TILE // CHAINS
 CHUNK, FINE = PART // 4, PART // 16
 ORDERS = ((4, 16, 1), (16, 1, 4), (1, 4, 16))
@@ -57,7 +58,7 @@
 
 
 def kernel(
-    one, two, scale_hbm, out, views, means, rests, held, held_means, own, other, inv_own, inv_other, part, got_a, sum_a, got_b, sum_b, got_c, full, gram, grads,
+    one, two, scale_hbm, out, views, means, rests, held, held_means, own, other, inv_own, inv_other, part, got_a, sum_a, got_b, sum_b, got_c, full, gram, products, grads,
     scale_ref, in_send, in_recv, mean_send, mean_recv, out_send, out_recv, pair_send, pair_recv, ring_send, ring_recv, local_sem, view_sem, scale_sem,
 ):
     chip, core = lax.axis_index("dp"), lax.axis_index("feat")
@@ -168,7 +169,7 @@
 
     def step(phase, q, hop, src, dst):
         stride = ORDERS[q % 3][(0, 1, 2, 1, 0)[phase]]
-        at = (phase * CHAINS + q) * 3 + hop - 1
+        at = phase * CHAINS + q
         return remote(src, dst, ring_send.at[at], ring_recv.at[at], partner(chip, stride, hop), core)
 
     def first(q, hop):
@@ -202,9 +203,13 @@
         for hop in HOPS:
             phase(q, hop).start()
 
+    def three(phase, q):
+        at = phase * CHAINS + q
+        all_three = (got_a, got_b, got_c, got_b, got_a)[phase].at[q]
+        return remote(all_three, all_three, ring_send.at[at], ring_recv.at[at], chip, core)
+
     def arrived(phase, q):
-        for hop in HOPS:
-            phase(q, hop).wait_recv()
+        three(phase, q).wait_recv()
 
     def summed(mine_ref, got, q):
         total = mine_ref.astype(F32)
@@ -253,34 +258,40 @@
 
     for wave in range(WAVES):
         for q in chains(wave):
-            arrived(first, q)
+            arrived(0, q)
             sum_a[q] = summed(part[chunk_rows(q), :], got_a, q)
             start(second, q)
     for wave in range(WAVES):
         for q in chains(wave):
-            arrived(second, q)
+            arrived(1, q)
             sum_b[q] = summed(sum_a[q, rows_at(coordinate(chip, ORDERS[q % 3][1]) * FINE, FINE), :], got_b, q)
             start(third, q)
     for wave in range(WAVES):
         for q in chains(wave):
-            arrived(third, q)
+            arrived(2, q)
             full[fine_rows(q), :] = summed(sum_b[q], got_c, q)
             start(fourth, q)
     for wave in range(WAVES):
         for q in chains(wave):
-            arrived(fourth, q)
+            arrived(3, q)
             start(fifth, q)
 
     for wave in range(WAVES):
         for q in chains(wave):
-            arrived(fifth, q)
+            arrived(4, q)
         for at, (r, c) in list(enumerate(BLOCKS))[wave * 36 // WAVES:(wave + 1) * 36 // WAVES]:
             block = full[at * TILE:(at + 1) * TILE, :]
             gram[r * TILE:(r + 1) * TILE, c * TILE:(c + 1) * TILE] = block
             if r != c:
                 gram[c * TILE:(c + 1) * TILE, r * TILE:(r + 1) * TILE] = block.T
+        since, until = WHOLE[wave], WHOLE[wave + 1]
+        rows = jnp.dot(gram[since:until, since:], other[since:, :], preferred_element_type=F32)
+        products[since:until, :] = rows if wave == 0 else products[since:until, :] + rows
+        if until < SAMPLES:
+            rest = jnp.dot(gram[until:, since:until], other[since:until, :], preferred_element_type=F32)
+            products[until:, :] = rest if wave == 0 else products[until:, :] + rest
     theirs = other[...].astype(F32)
-    back = jnp.dot(gram[...], other[...], preferred_element_type=F32) * (scale * (2.0 * offdiag_weight / (SAMPLES * SAMPLES)))
+    back = products[...] * (scale * (2.0 * offdiag_weight / (SAMPLES * SAMPLES)))
     back = back + own[...].astype(F32) * (diagonal / SAMPLES)
     weight = jnp.sum(back * theirs, axis=0, keepdims=True) / SAMPLES
     grads[...] = (inv_other[0:1, :] * (back - theirs * weight)).astype(BF16)
@@ -301,10 +312,9 @@
     def _():
         pltpu.make_async_copy(grads.at[rows_at(chip * ROWS, ROWS), :], place, local_sem.at[0]).start()
 
-    for phase in (first, second, third, fourth, fifth):
+    for phase in range(PHASES):
         for q in range(CHAINS):
-            for hop in HOPS:
-                phase(q, hop).wait_send()
+            three(phase, q).wait_send()
 
     @pl.when(mine)
     def _():
@@ -341,6 +351,7 @@
             pltpu.VMEM((CHAINS, 3, FINE, TILE), BF16),
             pltpu.VMEM((CHAINS * PART, TILE), BF16),
             pltpu.VMEM((SAMPLES, SAMPLES), BF16),
+            pltpu.VMEM((SAMPLES, TILE), F32),
             pltpu.VMEM((SAMPLES, TILE), BF16),
             pltpu.SMEM((1,), F32),
             pltpu.SemaphoreType.DMA,
@@ -351,8 +362,8 @@
             pltpu.SemaphoreType.DMA,
             pltpu.SemaphoreType.DMA((2,)),
             pltpu.SemaphoreType.DMA((2,)),
-            pltpu.SemaphoreType.DMA((PHASES * CHAINS * 3,)),
-            pltpu.SemaphoreType.DMA((PHASES * CHAINS * 3,)),
+            pltpu.SemaphoreType.DMA((PHASES * CHAINS,)),
+            pltpu.SemaphoreType.DMA((PHASES * CHAINS,)),
             pltpu.SemaphoreType.DMA((2,)),
             pltpu.SemaphoreType.DMA((2,)),
             pltpu.SemaphoreType.DMA,

time: 49.9 us -> 48.4 us (0.970)
  Pallas kernels: 47.6 us -> 46.1 us
    pallas_call x1, Pallas kernels: 47.6 us -> 46.1 us  [shards(): pl.pallas_call(kernel, out_shape=jax.ShapeDtypeStruct((2, ROWS, WIDE), BF...]
where the time goes in v4:
time: 48.4 us; the launch traced here: 48.2 us
  Pallas kernels  46.1 us (95%)
  between operations  1.28 us (3%)
  other arithmetic  0.83 us (2%)
    pallas_call x1, Pallas kernels, shards(): pl.pallas_call(kernel, out_shape=jax.ShapeDtypeStruct((2, ROWS, WIDE), BF...  46.1 us

profile of v4, /device:TPU:1, one launch (start us, length us, event | category | flops | bytes accessed | tf_op | source)
XLA Modules:
  0.0 48.2 jit_solution(18294076758156725570)
XLA Ops:
  1.3 46.1 %shard_map.50 = bf16[2,16,4096]{2,1,0:T(8,128)(2,1)S(1)} custom-call(f32[16,4096]{1,0:T(8,128)} %one.1, f32[16,4096]{1,0:T(8,128)} %two.1, f32[1]{0:T(128)S(6)} %copy.5.scale_hbm), custom_call_target="tpu_custom_call" | custom-call | tf_op jit(solution)/shard_map/pallas_call | solution.py:331
  47.4 0.8 %bitcast_convert_fusion = (f32[16,4096]{1,0:T(8,128)}, f32[16,4096]{1,0:T(8,128)}) fusion(bf16[2,16,4096]{2,1,0:T(8,128)(2,1)S(1)} %shard_map.50), kind=kLoop, calls=%fused_computation | loop fusion | flops 131072 | bytes 786432 | tf_op jit(solution)/shard_map/convert_element_type | solution.py:375

commit v5 on v4

--- a/solution.py
+++ b/solution.py
@@ -21,7 +21,7 @@
 CHUNK, FINE = PART // 4, PART // 16
 ORDERS = ((4, 16, 1), (16, 1, 4), (1, 4, 16))
 HOPS = (2, 1, 3)
-PHASES = 5
+PHASES = 7
 
 
 def apart(shift):
@@ -168,33 +168,44 @@
     swap_inv = remote(inv_own, inv_other, pair_send.at[1], pair_recv.at[1], chip, 1 - core)
 
     def step(phase, q, hop, src, dst):
-        stride = ORDERS[q % 3][(0, 1, 2, 1, 0)[phase]]
+        stride = ORDERS[q % 3][(0, 1, 2, 1, 0, 0, 0)[phase]]
         at = phase * CHAINS + q
         return remote(src, dst, ring_send.at[at], ring_recv.at[at], partner(chip, stride, hop), core)
 
+    def piece_rows(at, piece):
+        turn = coordinate(chip, ORDERS[at // 4 % 3][1])
+        return rows_at(at * TILE + (piece - turn + 4) % 4 * FINE, FINE)
+
+    def chunk_start(q, hop=0):
+        return q * PART + (coordinate(chip, ORDERS[q % 3][0]) + hop) % 4 * CHUNK
+
+    def own_rows(q, hop=0):
+        return rows_at(chunk_start(q, hop), FINE)
+
+    def further_rows(q, hop=0):
+        return rows_at(chunk_start(q, hop) + FINE, 3 * FINE)
+
     def first(q, hop):
-        to = (coordinate(chip, ORDERS[q % 3][0]) + hop) % 4
-        return step(0, q, hop, part.at[rows_at(q * PART + to * CHUNK, CHUNK), :], got_a.at[q, hop - 1])
+        return step(0, q, hop, part.at[further_rows(q, hop), :], got_a.at[q, hop - 1, FINE:CHUNK])
+
+    def first_own(q, hop):
+        return step(5, q, hop, part.at[own_rows(q, hop), :], got_a.at[q, hop - 1, 0:FINE])
 
     def second(q, hop):
-        to = (coordinate(chip, ORDERS[q % 3][1]) + hop) % 4
-        return step(1, q, hop, sum_a.at[q, rows_at(to * FINE, FINE), :], got_b.at[q, hop - 1])
+        return step(1, q, hop, sum_a.at[q, hop * FINE:(hop + 1) * FINE, :], got_b.at[q, hop - 1])
 
     def third(q, hop):
         return step(2, q, hop, sum_b.at[q], got_c.at[q, hop - 1])
 
-    def chunk_rows(q):
-        return rows_at(q * PART + coordinate(chip, ORDERS[q % 3][0]) * CHUNK, CHUNK)
-
-    def fine_rows(q):
-        start = q * PART + coordinate(chip, ORDERS[q % 3][0]) * CHUNK + coordinate(chip, ORDERS[q % 3][1]) * FINE
-        return rows_at(start, FINE)
-
     def fourth(q, hop):
-        return step(3, q, hop, full.at[fine_rows(q), :], full.at[fine_rows(q), :])
+        landing = rows_at(chunk_start(q) + (4 - hop) * FINE, FINE)
+        return step(3, q, hop, full.at[own_rows(q), :], full.at[landing, :])
+
+    def fourth_own(q, hop):
+        return step(6, q, hop, full.at[own_rows(q), :], full.at[own_rows(q), :])
 
     def fifth(q, hop):
-        return step(4, q, hop, full.at[chunk_rows(q), :], full.at[chunk_rows(q), :])
+        return step(4, q, hop, full.at[further_rows(q), :], full.at[further_rows(q), :])
 
     def chains(wave):
         return range(3 * wave, 3 * wave + 3)
@@ -205,16 +216,16 @@
 
     def three(phase, q):
         at = phase * CHAINS + q
-        all_three = (got_a, got_b, got_c, got_b, got_a)[phase].at[q]
+        all_three = part.at[0:9 * FINE, :] if phase in (0, 4) else got_b.at[q]
         return remote(all_three, all_three, ring_send.at[at], ring_recv.at[at], chip, core)
 
     def arrived(phase, q):
         three(phase, q).wait_recv()
 
-    def summed(mine_ref, got, q):
-        total = mine_ref.astype(F32)
-        for hop in HOPS:
-            total = total + got[q, hop - 1].astype(F32)
+    def summed(*terms):
+        total = terms[0].astype(F32)
+        for term in terms[1:]:
+            total = total + term.astype(F32)
         return total.astype(BF16)
 
 
@@ -243,10 +254,13 @@
                 )
                 for at, (row, c) in blocks:
                     if row == r:
-                        lanes = slice((c - columns[0]) * TILE, (c - columns[0] + 1) * TILE)
-                        part[at * TILE:(at + 1) * TILE, :] = panel[:, lanes].astype(BF16)
+                        block = panel[:, (c - columns[0]) * TILE:(c - columns[0] + 1) * TILE].astype(BF16)
+                        for k in range(4):
+                            part[piece_rows(at, k), :] = block[k * FINE:(k + 1) * FINE, :]
         for q in chains(wave):
             start(first, q)
+    for q in range(CHAINS):
+        start(first_own, q)
 
     sent_in()
     swap.wait()
@@ -256,31 +270,31 @@
     corr = jnp.sum(own[...].astype(F32) * other[...].astype(F32), axis=0, keepdims=True) / SAMPLES
     diagonal = scale * (2.0 * (corr - 1.0) - 2.0 * offdiag_weight * corr)
 
+    for q in range(CHAINS):
+        arrived(0, q)
+        further = slice(FINE, CHUNK)
+        sum_a[q, further] = summed(part[further_rows(q), :], *(got_a[q, k, further] for k in range(3)))
+        start(second, q)
+    for q in range(CHAINS):
+        arrived(5, q)
+        arrived(1, q)
+        sum_b[q] = summed(part[own_rows(q), :], *(got_a[q, k, 0:FINE] for k in range(3)), *(got_b[q, k] for k in range(3)))
+        start(third, q)
+    for q in range(CHAINS):
+        arrived(2, q)
+        full[own_rows(q), :] = summed(sum_b[q], *(got_c[q, k] for k in range(3)))
+        start(fourth, q)
+        start(fourth_own, q)
+    for q in range(CHAINS):
+        arrived(3, q)
+        start(fifth, q)
+
     for wave in range(WAVES):
         for q in chains(wave):
-            arrived(0, q)
-            sum_a[q] = summed(part[chunk_rows(q), :], got_a, q)
-            start(second, q)
-    for wave in range(WAVES):
-        for q in chains(wave):
-            arrived(1, q)
-            sum_b[q] = summed(sum_a[q, rows_at(coordinate(chip, ORDERS[q % 3][1]) * FINE, FINE), :], got_b, q)
-            start(third, q)
-    for wave in range(WAVES):
-        for q in chains(wave):
-            arrived(2, q)
-            full[fine_rows(q), :] = summed(sum_b[q], got_c, q)
-            start(fourth, q)
-    for wave in range(WAVES):
-        for q in chains(wave):
-            arrived(3, q)
-            start(fifth, q)
-
-    for wave in range(WAVES):
-        for q in chains(wave):
+            arrived(6, q)
             arrived(4, q)
         for at, (r, c) in list(enumerate(BLOCKS))[wave * 36 // WAVES:(wave + 1) * 36 // WAVES]:
-            block = full[at * TILE:(at + 1) * TILE, :]
+            block = jnp.concatenate([full[piece_rows(at, k), :] for k in range(4)], axis=0)
             gram[r * TILE:(r + 1) * TILE, c * TILE:(c + 1) * TILE] = block
             if r != c:
                 gram[c * TILE:(c + 1) * TILE, r * TILE:(r + 1) * TILE] = block.T
@@ -301,8 +315,11 @@
     def to_samples(chip_to):
         return remote(grads.at[rows_at(chip_to * ROWS, ROWS), :], place, out_send, out_recv, chip_to, half)
 
-    for shift in SHIFTS[:-1]:
-        to_samples(shifted(shift)).start()
+    for y in range(4):
+        for x, z in PLANE[:-1]:
+            to_samples(y * 16 + (at_x + x) % 4 * 4 + (at_z + z) % 4).start()
+    for dy in (2, 1, 3):
+        to_samples(shifted((dy, 0, 0))).start()
 
     @pl.when(not_mine)
     def _():

time: 48.4 us -> 47.8 us (0.988)
  Pallas kernels: 46.1 us -> 45.6 us
    pallas_call x1, Pallas kernels: 46.1 us -> 45.6 us  [shards(): pl.pallas_call(kernel, out_shape=jax.ShapeDtypeStruct((2, ROWS, WIDE), BF...]
where the time goes in v5:
time: 47.8 us; the launch traced here: 47.7 us
  Pallas kernels  45.6 us (95%)
  between operations  1.28 us (3%)
  other arithmetic  0.83 us (2%)
    pallas_call x1, Pallas kernels, shards(): pl.pallas_call(kernel, out_shape=jax.ShapeDtypeStruct((2, ROWS, WIDE), BF...  45.6 us

profile of v5, /device:TPU:1, one launch (start us, length us, event | category | flops | bytes accessed | tf_op | source)
XLA Modules:
  0.0 47.7 jit_solution(15289500553092417256)
XLA Ops:
  1.3 45.6 %shard_map.50 = bf16[2,16,4096]{2,1,0:T(8,128)(2,1)S(1)} custom-call(f32[16,4096]{1,0:T(8,128)} %one.1, f32[16,4096]{1,0:T(8,128)} %two.1, f32[1]{0:T(128)S(6)} %copy.5.scale_hbm), custom_call_target="tpu_custom_call" | custom-call | tf_op jit(solution)/shard_map/pallas_call | solution.py:348
  46.9 0.8 %bitcast_convert_fusion = (f32[16,4096]{1,0:T(8,128)}, f32[16,4096]{1,0:T(8,128)}) fusion(bf16[2,16,4096]{2,1,0:T(8,128)(2,1)S(1)} %shard_map.50), kind=kLoop, calls=%fused_computation | loop fusion | flops 131072 | bytes 786432 | tf_op jit(solution)/shard_map/convert_element_type | solution.py:392

commit v6 on v5

--- a/solution.py
+++ b/solution.py
@@ -21,7 +21,7 @@
 CHUNK, FINE = PART // 4, PART // 16
 ORDERS = ((4, 16, 1), (16, 1, 4), (1, 4, 16))
 HOPS = (2, 1, 3)
-PHASES = 7
+PHASES = 5
 
 
 def apart(shift):
@@ -90,9 +90,10 @@
         load.wait()
         samples = views[k]
         block_mean = jnp.sum(samples, axis=0, keepdims=True) / ROWS
-        rests[k] = (samples - block_mean).astype(BF16)
+        rest = (samples - block_mean).astype(BF16)
         for t in range(WIDE // TILE):
             means[k, t] = block_mean[:, t * TILE:(t + 1) * TILE]
+            rests[k, t] = rest[:, t * TILE:(t + 1) * TILE]
 
     @pl.when(mine)
     def _():
@@ -108,13 +109,13 @@
         t = chip_to % 32
         return (
             remote(means.at[core_to, t], held_means.at[chip], mean_send, mean_recv, chip_to, core_to),
-            remote(rests.at[core_to, :, lanes_at(t)], my_rows, in_send, in_recv, chip_to, core_to),
+            remote(rests.at[core_to, t], my_rows, in_send, in_recv, chip_to, core_to),
         )
 
     def stay_here():
         return (
             pltpu.make_async_copy(means.at[core, tile], held_means.at[chip], local_sem.at[0]),
-            pltpu.make_async_copy(rests.at[core, :, lanes_at(tile)], my_rows, local_sem.at[1]),
+            pltpu.make_async_copy(rests.at[core, tile], my_rows, local_sem.at[1]),
         )
 
     for x, z in PLANE[:-1]:
@@ -169,8 +170,8 @@
 
     def step(phase, q, hop, src, dst):
         stride = ORDERS[q % 3][(0, 1, 2, 1, 0, 0, 0)[phase]]
-        at = phase * CHAINS + q
-        return remote(src, dst, ring_send.at[at], ring_recv.at[at], partner(chip, stride, hop), core)
+        at = (0, 1, 2, 3, 4, 1, 4)[phase] * CHAINS + q
+        return remote(src, dst, ring_send.at[q], ring_recv.at[at], partner(chip, stride, hop), core)
 
     def piece_rows(at, piece):
         turn = coordinate(chip, ORDERS[at // 4 % 3][1])
@@ -214,13 +215,12 @@
         for hop in HOPS:
             phase(q, hop).start()
 
-    def three(phase, q):
-        at = phase * CHAINS + q
-        all_three = part.at[0:9 * FINE, :] if phase in (0, 4) else got_b.at[q]
-        return remote(all_three, all_three, ring_send.at[at], ring_recv.at[at], chip, core)
+    def waits(phase, q, pieces):
+        rows = part.at[0:pieces * FINE, :]
+        return remote(rows, rows, ring_send.at[q], ring_recv.at[phase * CHAINS + q], chip, core)
 
     def arrived(phase, q):
-        three(phase, q).wait_recv()
+        waits(phase, q, (9, 6, 3, 3, 12)[phase]).wait_recv()
 
     def summed(*terms):
         total = terms[0].astype(F32)
@@ -276,7 +276,6 @@
         sum_a[q, further] = summed(part[further_rows(q), :], *(got_a[q, k, further] for k in range(3)))
         start(second, q)
     for q in range(CHAINS):
-        arrived(5, q)
         arrived(1, q)
         sum_b[q] = summed(part[own_rows(q), :], *(got_a[q, k, 0:FINE] for k in range(3)), *(got_b[q, k] for k in range(3)))
         start(third, q)
@@ -291,7 +290,6 @@
 
     for wave in range(WAVES):
         for q in chains(wave):
-            arrived(6, q)
             arrived(4, q)
         for at, (r, c) in list(enumerate(BLOCKS))[wave * 36 // WAVES:(wave + 1) * 36 // WAVES]:
             block = jnp.concatenate([full[piece_rows(at, k), :] for k in range(4)], axis=0)
@@ -329,9 +327,8 @@
     def _():
         pltpu.make_async_copy(grads.at[rows_at(chip * ROWS, ROWS), :], place, local_sem.at[0]).start()
 
-    for phase in range(PHASES):
-        for q in range(CHAINS):
-            three(phase, q).wait_send()
+    for q in range(CHAINS):
+        waits(0, q, 33).wait_send()
 
     @pl.when(mine)
     def _():
@@ -353,7 +350,7 @@
         scratch_shapes=[
             pltpu.VMEM((2, ROWS, WIDE), F32),
             pltpu.VMEM((2, WIDE // TILE, 1, TILE), F32),
-            pltpu.VMEM((2, ROWS, WIDE), BF16),
+            pltpu.VMEM((2, WIDE // TILE, ROWS, TILE), BF16),
             pltpu.VMEM((SAMPLES, TILE), BF16),
             pltpu.VMEM((CHIPS, 1, TILE), F32),
             pltpu.VMEM((SAMPLES, TILE), BF16),
@@ -379,7 +376,7 @@
             pltpu.SemaphoreType.DMA,
             pltpu.SemaphoreType.DMA((2,)),
             pltpu.SemaphoreType.DMA((2,)),
-            pltpu.SemaphoreType.DMA((PHASES * CHAINS,)),
+            pltpu.SemaphoreType.DMA((CHAINS,)),
             pltpu.SemaphoreType.DMA((PHASES * CHAINS,)),
             pltpu.SemaphoreType.DMA((2,)),
             pltpu.SemaphoreType.DMA((2,)),

time: 47.8 us -> 47.2 us (0.987)
  Pallas kernels: 45.6 us -> 44.9 us
    pallas_call x1, Pallas kernels: 45.6 us -> 44.9 us  [shards(): pl.pallas_call(kernel, out_shape=jax.ShapeDtypeStruct((2, ROWS, WIDE), BF...]
where the time goes in v6:
time: 47.2 us; the launch traced here: 47.1 us
  Pallas kernels  44.9 us (95%)
  between operations  1.28 us (3%)
  other arithmetic  0.83 us (2%)
    pallas_call x1, Pallas kernels, shards(): pl.pallas_call(kernel, out_shape=jax.ShapeDtypeStruct((2, ROWS, WIDE), BF...  44.9 us

profile of v6, /device:TPU:1, one launch (start us, length us, event | category | flops | bytes accessed | tf_op | source)
XLA Modules:
  0.0 47.1 jit_solution(1033603329950985051)
XLA Ops:
  1.3 44.9 %shard_map.50 = bf16[2,16,4096]{2,1,0:T(8,128)(2,1)S(1)} custom-call(f32[16,4096]{1,0:T(8,128)} %one.1, f32[16,4096]{1,0:T(8,128)} %two.1, f32[1]{0:T(128)S(6)} %copy.5.scale_hbm), custom_call_target="tpu_custom_call" | custom-call | tf_op jit(solution)/shard_map/pallas_call | solution.py:345
  46.2 0.8 %bitcast_convert_fusion = (f32[16,4096]{1,0:T(8,128)}, f32[16,4096]{1,0:T(8,128)}) fusion(bf16[2,16,4096]{2,1,0:T(8,128)(2,1)S(1)} %shard_map.50), kind=kLoop, calls=%fused_computation | loop fusion | flops 131072 | bytes 786432 | tf_op jit(solution)/shard_map/convert_element_type | solution.py:389

commit v7 on v6

--- a/solution.py
+++ b/solution.py
@@ -306,7 +306,7 @@
     back = products[...] * (scale * (2.0 * offdiag_weight / (SAMPLES * SAMPLES)))
     back = back + own[...].astype(F32) * (diagonal / SAMPLES)
     weight = jnp.sum(back * theirs, axis=0, keepdims=True) / SAMPLES
-    grads[...] = (inv_other[0:1, :] * (back - theirs * weight)).astype(BF16)
+    gain = inv_other[0:1, :]
 
     place = out.at[1 - core, :, lanes_at(tile)]
 
@@ -314,6 +314,8 @@
         return remote(grads.at[rows_at(chip_to * ROWS, ROWS), :], place, out_send, out_recv, chip_to, half)
 
     for y in range(4):
+        quarter = slice(y * SAMPLES // 4, (y + 1) * SAMPLES // 4)
+        grads[quarter, :] = (gain * (back[quarter, :] - theirs[quarter, :] * weight)).astype(BF16)
         for x, z in PLANE[:-1]:
             to_samples(y * 16 + (at_x + x) % 4 * 4 + (at_z + z) % 4).start()
     for dy in (2, 1, 3):

time: 47.2 us -> 47.1 us (level)
  no operation moved by 1% of the time
where the time goes in v7:
time: 47.1 us; the launch traced here: 47 us
  Pallas kernels  44.9 us (95%)
  between operations  1.28 us (3%)
  other arithmetic  0.83 us (2%)
    pallas_call x1, Pallas kernels, shards(): pl.pallas_call(kernel, out_shape=jax.ShapeDtypeStruct((2, ROWS, WIDE), BF...  44.9 us

profile of v7, /device:TPU:1, one launch (start us, length us, event | category | flops | bytes accessed | tf_op | source)
XLA Modules:
  0.0 47.0 jit_solution(16471728683178725668)
XLA Ops:
  1.3 44.9 %shard_map.50 = bf16[2,16,4096]{2,1,0:T(8,128)(2,1)S(1)} custom-call(f32[16,4096]{1,0:T(8,128)} %one.1, f32[16,4096]{1,0:T(8,128)} %two.1, f32[1]{0:T(128)S(6)} %copy.5.scale_hbm), custom_call_target="tpu_custom_call" | custom-call | tf_op jit(solution)/shard_map/pallas_call | solution.py:347
  46.1 0.8 %bitcast_convert_fusion = (f32[16,4096]{1,0:T(8,128)}, f32[16,4096]{1,0:T(8,128)}) fusion(bf16[2,16,4096]{2,1,0:T(8,128)(2,1)S(1)} %shard_map.50), kind=kLoop, calls=%fused_computation | loop fusion | flops 131072 | bytes 786432 | tf_op jit(solution)/shard_map/convert_element_type | solution.py:391
